TPU v7x, 32 devices: a whole 2x2x4 slice. The times are simulated.
32 devices in a mesh: seq: 8 (over z, y), head: 4 (over x, core).
Axes of the slice: x: 2, y: 2, z: 4, core: 2. Of those that a mesh axis runs over, the one named last changes fastest.
Arguments:
- tokens: bfloat16 [6144, 4096], P('seq'), may hold values from -6 to 6
- w_qkv: bfloat16 [3, 4096, 4096], P(None, 'seq', 'head'), may hold values from -0.09375 to 0.09375
- w_out: bfloat16 [4096, 4096], P('head', 'seq'), may hold values from -0.09375 to 0.09375
- prior_state: float32 [32, 128, 128], P('head'), may hold values from -384 to 384
- norm_gain: float32 [4096], P('head'), may hold values from 0.1 to 1.9
Outputs:
- mixed: bfloat16 [6144, 4096], P('seq', 'head')
All inputs are finite; a program needn't handle non-finite values.
Results may differ from a plain program's by a relative error of at most 0.013.
Values may be sent and summed in bfloat16 or wider, within the bound.
A program may use at most 128 MiB of HBM per device.

v0:
```python
import jax
import jax.numpy as jnp
from jax import lax
from jax.sharding import PartitionSpec as P

HEAD_DIM = 128


def prefix_2(x, axis, combine, identity):
    length, here = (lax.axis_size(axis), lax.axis_index(axis))
    everything = lax.all_gather(x.astype(jnp.bfloat16), axis)
    start = jnp.broadcast_to(jnp.asarray(identity, x.dtype), x.shape)

    def turn(k, before):
        reached = k < here
        new = combine(before, everything[k].astype(x.dtype))
        return jnp.where(reached, new, before)

    return lax.fori_loop(0, length, turn, start)


def per_device(tokens, w_qkv, w_out, prior_state, norm_gain):
    f32 = jnp.float32
    rows = tokens.shape[0]
    cols = w_qkv.shape[2]
    heads = cols // HEAD_DIM
    proj = jnp.einsum(
        "td,cde->cte",
        tokens,
        lax.all_gather(w_qkv, "seq", axis=1, tiled=True),
        preferred_element_type=f32,
    )
    query = jax.nn.silu(proj[0]).astype(jnp.bfloat16).reshape(rows, heads, HEAD_DIM)
    key = jax.nn.silu(proj[1]).astype(jnp.bfloat16).reshape(rows, heads, HEAD_DIM)
    value = proj[2].astype(jnp.bfloat16).reshape(rows, heads, HEAD_DIM)
    local = jnp.einsum("thi,thj->hij", key, value, preferred_element_type=f32)
    earlier = prefix_2(local, "seq", lambda first, second: first + second, jnp.zeros_like(local))
    prefix = prior_state + earlier
    scores = jnp.einsum("thi,shi->hts", query, key, preferred_element_type=f32)
    place = jnp.arange(rows)
    keep = place[None, :] <= place[:, None]
    scores = jnp.where(keep[None], scores, 0.0).astype(jnp.bfloat16)
    inner = jnp.einsum("hts,shj->thj", scores, value, preferred_element_type=f32)
    outer = jnp.einsum("thi,hij->thj", query.astype(f32), prefix, precision=lax.Precision.HIGHEST)
    attended = inner + outer
    scale = lax.rsqrt(jnp.mean(attended * attended, axis=2, keepdims=True) + 1e-06)
    normed = (
        (attended * scale * norm_gain.reshape(heads, HEAD_DIM))
        .astype(jnp.bfloat16)
        .reshape(rows, cols)
    )
    partial_value = jnp.dot(
        normed, lax.all_gather(w_out, "seq", axis=1, tiled=True), preferred_element_type=f32
    )
    return lax.psum_scatter(
        partial_value.astype(jnp.bfloat16), "head", scatter_dimension=1, tiled=True
    )


def solution(mesh):
    in_specs = (
        P("seq", None),
        P(None, "seq", "head"),
        P("head", "seq"),
        P("head", None, None),
        P("head"),
    )
    out_specs = P("seq", "head")
    return jax.shard_map(
        per_device, mesh=mesh, in_specs=in_specs, out_specs=out_specs, check_vma=False
    )
```

profile of v0, /device:TPU:0, one launch (start us, length us, event | category | flops | bytes accessed | tf_op | source)
XLA Modules:
  0.0 780.2 jit_solution(7017793307484028102)
XLA Ops:
  6.5 0.0 all-gather.5.cloned.1.call-start
  6.5 4.6 copy.14
  11.2 0.0 all-gather.5.cloned.1.call-update
  11.2 0.0 all-gather.9.cloned.1.call-start
  11.3 483.2 %all-gather.5.cloned.1.call-done = bf16[3,4096,1024]{1,2,0:T(8,128)(2,1)} async-done(((bf16[3,512,1024]{1,2,0:T(8,128)(2,1)}), bf16[3,4096,1024]{1,2,0:T(8,128)(2,1)}) %all-gather.5.cloned.1.call-update) | async-done | bytes 25165840 | tf_op jit(solution)/shard_map/all_gather | solution.py:30
  494.5 24.9 %fusion.7 = f32[3,768,1024]{1,2,0:T(8,128)S(1)} fusion(bf16[3,4096,1024]{1,2,0:T(8,128)(2,1)} %all-gather.5.cloned.1.call-done, bf16[768,4096]{1,0:T(8,128)(2,1)} %param.7), kind=kOutput, calls=%fused_computation.9 | convolution fusion | flops 19327352832 | bytes 40894464 | tf_op jit(solution)/shard_map/td,cde->cte/dot_general | solution.py:27
  519.5 2.1 fusion.15
  521.6 1.3 slice.17
  522.9 2.3 copy.18
  525.2 4.1 convolution_convert_fusion.1
  529.3 0.0 all-gather.9.cloned.1.call-update
  529.3 0.0 all-gather.7.cloned.1.call-start
  529.4 0.7 all-gather.7.cloned.1.call-update
  530.1 0.2 reduce-scatter.2.cloned.1.call-start
  530.3 0.2 iota_compare_fusion
  530.5 0.0 copy-start
  530.5 3.7 copy.16
  534.2 0.0 copy-done
  534.2 10.4 %fusion = f32[8,128,768]{2,1,0:T(8,128)} fusion(bf16[768,8,128]{0,2,1:T(8,128)(2,1)S(1)} %bitcast.35, pred[768,768]{1,0:T(8,128)(4,1)S(1)} %iota_compare_fusion, f32[768,8,128]{2,0,1:T(8,128)} %copy.16, f32[768,8,128]{2,0,1:T(8,128)} %copy.18), kind=kOutput, calls=%fused_computation.2 | convolution fusion | flops 2433220608 | bytes 11599872 | tf_op jit(solution)/shard_map/hts,shj->thj/dot_general | solution.py:43
  544.6 34.3 %all-gather.9.cloned.1.call-done = bf16[64,128,128]{2,1,0:T(8,128)(2,1)} async-done(((bf16[8,128,128]{2,1,0:T(8,128)(2,1)}), bf16[64,128,128]{2,1,0:T(8,128)(2,1)}) %all-gather.9.cloned.1.call-update) | async-done | bytes 2097168 | tf_op jit(solution)/shard_map/all_gather | solution.py:11
  578.9 0.0 copy-start.2
  578.9 10.2 %while.14 = (s32[]{:T(128)}, f32[8,128,128]{2,1,0:T(8,128)S(1)}, s32[]{:T(128)}, bf16[8,8,128,128]{3,2,1,0:T(8,128)(2,1)}, s32[]{:T(128)}, /*index=5*/s32[]{:T(128)}) while((s32[]{:T(128)}, f32[8,128,128]{2,1,0:T(8,128)S(1)}, s32[]{:T(128)}, bf16[8,8,128,128]{3,2,1,0:T(8,128)(2,1)}, s32[]{:T(128)}, /*index=5*/s32[]{:T(128)}) %tuple.45), condition=%wide.region_1.2_spmd.clone, body=%wide.region_0.1_spmd.clone.sunk | while | flops 524292 | bytes 1310813 | solution.py:19
  578.9 1.3 add_select_fusion.2
  580.2 1.2 add_select_fusion.2
  581.5 1.2 add_select_fusion.2
  582.7 1.2 add_select_fusion.2
  584.0 1.2 add_select_fusion.2
  585.2 1.2 add_select_fusion.2
  586.5 1.3 add_select_fusion.2
  587.8 1.3 add_select_fusion.2
  589.1 0.0 copy-done.2
  589.1 0.0 copy-start.1
  589.1 5.4 fusion.10
  594.5 0.0 copy-done.1
  594.5 0.4 fusion.12
  594.8 110.0 %all-gather.7.cloned.1.call-done = bf16[1024,4096]{1,0:T(8,128)(2,1)} async-done(((bf16[1024,512]{1,0:T(8,128)(2,1)}), bf16[1024,4096]{1,0:T(8,128)(2,1)}) %all-gather.7.cloned.1.call-update) | async-done | bytes 8388624 | tf_op jit(solution)/shard_map/all_gather | solution.py:53
  704.8 12.1 %convolution_convert_fusion = bf16[768,4096]{1,0:T(8,128)(2,1)} fusion(bf16[768,1024]{0,1:T(8,128)(2,1)S(1)} %bitcast.36, bf16[1024,4096]{1,0:T(8,128)(2,1)} %all-gather.7.cloned.1.call-done), kind=kOutput, calls=%fused_computation.5 | convolution fusion | flops 6445596672 | bytes 16252928 | tf_op jit(solution)/shard_map/dot_general | solution.py:52
  716.9 0.0 reduce-scatter.2.cloned.1.call-update
  717.0 56.7 %reduce-scatter.2.cloned.1.call-done = bf16[768,1024]{1,0:T(8,128)(2,1)} async-done(((bf16[768,4096]{1,0:T(8,128)(2,1)}), bf16[768,1024]{1,0:T(8,128)(2,1)}) %reduce-scatter.2.cloned.1.call-update) | async-done | bytes 1572880 | tf_op jit(solution)/shard_map/reduce_scatter | solution.py:55
  (2 shorter events, 0.0 us)
Async XLA Ops:
  6.5 488.0 %all-gather.5.cloned.1.call-start = ((), (), s32[]{:S(2)}) async-start(), calls=%async_computation.1 | async-start | bytes 28311552 | tf_op jit(solution)/shard_map/all_gather | solution.py:30
  11.2 567.7 %all-gather.9.cloned.1.call-start = ((), (), s32[]{:S(2)}) async-start(), calls=%async_computation.4 | async-start | bytes 2359296 | tf_op jit(solution)/shard_map/all_gather | solution.py:11
  529.3 175.5 %all-gather.7.cloned.1.call-start = ((), (), s32[]{:S(2)}) async-start(), calls=%async_computation.2 | async-start | bytes 9437184 | tf_op jit(solution)/shard_map/all_gather | solution.py:53
  530.1 243.6 %reduce-scatter.2.cloned.1.call-start = ((), (), s32[]{:S(2)}) async-start(), calls=%async_computation.3 | async-start | bytes 7864320 | tf_op jit(solution)/shard_map/reduce_scatter | solution.py:55
  530.5 3.7 copy-start
  578.9 10.2 %copy-start.2 = (f32[8,128,128]{2,1,0:T(8,128)S(1)}, f32[8,128,128]{2,1,0:T(8,128)}, u32[]{:S(2)}) copy-start(f32[8,128,128]{2,1,0:T(8,128)} %param.10) | copy-start | bytes 1572868
  589.1 5.4 copy-start.1
Sparse Core Ops, SparseCore 0:
  11.3 483.1 all-gather.4
  529.4 49.3 all-gather.8
  580.9 123.8 all-gather.6
  717.1 56.5 reduce-scatter.1
where the time goes:
time: 781 us; the launch traced here: 780 us
  waiting for transfers between devices  685 us (88%)
  matrix products  56.9 us (7%)
  local copies, waits for them, and re-layouts  14.1 us (2%)
  between operations  13.2 us (2%)
  other arithmetic  10.6 us (1%)
    all_gather x1, waiting for transfers between devices, per_device(): lax.all_gather(w_qkv, 'seq', axis=1, tiled=True)  483 us
    all_gather x1, waiting for transfers between devices, per_device(): lax.all_gather(w_out, 'seq', axis=1, tiled=True)  110 us
    reduce_scatter x1, waiting for transfers between devices, per_device(): lax.psum_scatter(partial_value.astype(jnp.bfloat16), 'head', scatter_dime...  56.7 us
    all_gather x1, waiting for transfers between devices, prefix_2(): everything = lax.all_gather(x.astype(jnp.bfloat16), axis)  34.3 us
    dot_general x1, matrix products, per_device(): jnp.einsum('td,cde->cte', tokens, lax.all_gather(w_qkv, 'seq', axis=1, ti...  24.9 us
  transfers between devices with their start and end apart: 4, of which 4 were waited for; matrix products, arithmetic and copies ran while one was open for 4% of the time, Pallas kernels for 0%

commit v1 on v0

v1 whole, which is shorter than its diff:
```python
import functools

import jax
import jax.numpy as jnp
from jax import lax
from jax.experimental import pallas as pl
from jax.experimental.pallas import tpu as pltpu
from jax.sharding import PartitionSpec as P

HEAD_DIM = 128
MESH = pl.DeviceIdType.MESH


def gather_kernel(n, pieces, arrays, *refs):
    ins, outs = refs[:arrays], refs[arrays : 2 * arrays]
    send_sem, recv_sem, local_sem = refs[2 * arrays :]
    me = lax.axis_index("seq")
    length = n // 2
    row, side = me // 2, me % 2
    pair = row * 2 + 1 - side
    has_left, has_right = row > 0, row < length - 1
    left, right = me - 2, me + 2

    barrier = pltpu.get_barrier_semaphore()
    pl.semaphore_signal(barrier, inc=1, device_id={"seq": pair}, device_id_type=MESH)

    @pl.when(has_left)
    def _():
        pl.semaphore_signal(barrier, inc=1, device_id={"seq": left}, device_id_type=MESH)

    @pl.when(has_right)
    def _():
        pl.semaphore_signal(barrier, inc=1, device_id={"seq": right}, device_id_type=MESH)

    pl.semaphore_wait(barrier, 1 + has_left.astype(jnp.int32) + has_right.astype(jnp.int32))

    def copy(owner, piece, way, own=False):
        array, source, target, _ = pieces[piece]
        place = outs[array].at[target(owner)]
        return pltpu.make_async_remote_copy(
            src_ref=ins[array].at[source] if own else place,
            dst_ref=place,
            send_sem=send_sem.at[way, owner, piece],
            recv_sem=recv_sem.at[owner, piece],
            device_id={"seq": (left, right, pair)[way]},
            device_id_type=MESH,
        )

    def along(step, received, act):
        for piece, (_, _, _, cross) in enumerate(pieces):
            for lane in range(2 if cross else 1):
                off = side if lane == 0 else 1 - side
                for way, owner_row, there, further in (
                    (1, row - step, row >= step, has_right),
                    (0, row + step, row + step < length, has_left),
                ):
                    owner = owner_row * 2 + off

                    @pl.when(there)
                    def _():
                        if received:
                            copy(owner, piece, 2).wait_recv()
                        if not cross:
                            act(copy(owner, piece, 2))

                        @pl.when(further)
                        def _():
                            act(copy(owner, piece, way))

    def begin(act):
        for piece, (_, _, _, cross) in enumerate(pieces):
            act(copy(me, piece, 2, True))

            @pl.when(has_left)
            def _():
                act(copy(me, piece, 0, True))

            @pl.when(has_right)
            def _():
                act(copy(me, piece, 1, True))

    def crossed(received, act):
        for piece, (_, _, _, cross) in enumerate(pieces):
            if cross:
                if received:
                    copy(pair, piece, 2).wait_recv()

                @pl.when(has_left)
                def _():
                    act(copy(pair, piece, 0))

                @pl.when(has_right)
                def _():
                    act(copy(pair, piece, 1))

    locals_ = [
        pltpu.make_async_copy(
            ins[array].at[source], outs[array].at[target(me)], local_sem.at[piece]
        )
        for piece, (array, source, target, _) in enumerate(pieces)
    ]
    begin(lambda c: c.start())
    for c in locals_:
        c.start()
    crossed(True, lambda c: c.start())

    @pl.loop(1, length)
    def _(step):
        along(step, True, lambda c: c.start())

    @pl.loop(0, length)
    def _(other):
        owner = other * 2 + 1 - side
        for piece, (_, _, _, cross) in enumerate(pieces):
            if not cross:
                copy(owner, piece, 2).wait_recv()

    begin(lambda c: c.wait_send())
    for c in locals_:
        c.wait()
    crossed(False, lambda c: c.wait_send())

    @pl.loop(1, length)
    def _(step):
        along(step, False, lambda c: c.wait_send())


def gather(n, identity, pieces, shapes, *blocks):
    count = len(pieces)
    anywhere = pl.BlockSpec(memory_space=pl.ANY)
    return pl.pallas_call(
        functools.partial(gather_kernel, n, pieces, len(blocks)),
        out_shape=[jax.ShapeDtypeStruct(s, b.dtype) for s, b in zip(shapes, blocks)],
        in_specs=[anywhere] * len(blocks),
        out_specs=[anywhere] * len(blocks),
        scratch_shapes=[
            pltpu.SemaphoreType.DMA((3, n, count)),
            pltpu.SemaphoreType.DMA((n, count)),
            pltpu.SemaphoreType.DMA((count,)),
        ],
        compiler_params=pltpu.CompilerParams(collective_id=identity, has_side_effects=True),
    )(*blocks)


def gather_weights(w_qkv, w_out):
    n = lax.axis_size("seq")
    _, depth, cols = w_qkv.shape
    rows, width = w_out.shape
    half, quarter = depth // 2, rows // 4
    pieces = []

    def rows_piece(c, part, cross):
        pieces.append((
            0,
            (c, pl.ds(part * half, half)),
            lambda owner: (c, pl.ds(pl.multiple_of(owner * depth + part * half, half), half)),
            cross,
        ))

    def cols_piece(part, cross):
        span = pl.ds(part * quarter, quarter)
        pieces.append((
            1,
            (span,),
            lambda owner: (span, pl.ds(pl.multiple_of(owner * width, width), width)),
            cross,
        ))

    for c in range(3):
        for part in range(2):
            rows_piece(c, part, c == 0 and part == 0)
    for part in range(4):
        cols_piece(part, part == 0)
    shapes = ((3, n * depth, cols), (rows, n * width))
    return gather(n, 0, pieces, shapes, w_qkv, w_out)


def gather_states(states):
    n = lax.axis_size("seq")
    heads = states.shape[0]
    each = heads // 4
    pieces = [
        (
            0,
            (pl.ds(part * each, each),),
            lambda owner, part=part: (owner, pl.ds(part * each, each)),
            part == 0,
        )
        for part in range(4)
    ]
    return gather(n, 1, pieces, ((n, *states.shape),), states)[0]


def per_device(tokens, w_qkv, w_out, prior_state, norm_gain):
    f32 = jnp.float32
    rows = tokens.shape[0]
    cols = w_qkv.shape[2]
    heads = cols // HEAD_DIM
    w_all, w_out_all = gather_weights(w_qkv, w_out)
    proj = jnp.einsum("td,cde->cte", tokens, w_all, preferred_element_type=f32)
    query = jax.nn.silu(proj[0]).astype(jnp.bfloat16).reshape(rows, heads, HEAD_DIM)
    key = jax.nn.silu(proj[1]).astype(jnp.bfloat16).reshape(rows, heads, HEAD_DIM)
    value = proj[2].astype(jnp.bfloat16).reshape(rows, heads, HEAD_DIM)
    local = jnp.einsum("thi,thj->hij", key, value, preferred_element_type=f32)
    states = gather_states(local.astype(jnp.bfloat16))
    before = jnp.arange(states.shape[0]) < lax.axis_index("seq")
    earlier = jnp.sum(
        jnp.where(before[:, None, None, None], states.astype(f32), 0.0), axis=0
    )
    prefix = prior_state + earlier
    scores = jnp.einsum("thi,shi->hts", query, key, preferred_element_type=f32)
    place = jnp.arange(rows)
    keep = place[None, :] <= place[:, None]
    scores = jnp.where(keep[None], scores, 0.0).astype(jnp.bfloat16)
    inner = jnp.einsum("hts,shj->thj", scores, value, preferred_element_type=f32)
    outer = jnp.einsum("thi,hij->thj", query.astype(f32), prefix, precision=lax.Precision.HIGHEST)
    attended = inner + outer
    scale = lax.rsqrt(jnp.mean(attended * attended, axis=2, keepdims=True) + 1e-06)
    normed = (
        (attended * scale * norm_gain.reshape(heads, HEAD_DIM))
        .astype(jnp.bfloat16)
        .reshape(rows, cols)
    )
    partial_value = jnp.dot(normed, w_out_all, preferred_element_type=f32)
    return lax.psum_scatter(
        partial_value.astype(jnp.bfloat16), "head", scatter_dimension=1, tiled=True
    )


def solution(mesh):
    in_specs = (
        P("seq", None),
        P(None, "seq", "head"),
        P("head", "seq"),
        P("head", None, None),
        P("head"),
    )
    out_specs = P("seq", "head")
    return jax.shard_map(
        per_device, mesh=mesh, in_specs=in_specs, out_specs=out_specs, check_vma=False
    )
```

time: 781 us -> 501 us (0.64)
  waiting for transfers between devices: 685 us -> 58.8 us
  Pallas kernels: 0 us -> 363 us
  other arithmetic: 10.6 us -> 1.89 us
    all_gather x3 -> x0, waiting for transfers between devices: 628 us -> none  [the longest x1 483 us: per_device(): lax.all_gather(w_qkv, 'seq', axis=1, tiled=True)]
    pallas_call x0 -> x2, Pallas kernels: none -> 363 us  [gather(): pl.pallas_call(functools.partial(gather_kernel, n, pieces, len(blocks)),...]
    select_n x8 -> x0, other arithmetic: 9.99 us -> none  [turn(): return jnp.where(reached, new, before)]
  transfers between devices with their start and end apart: 4 -> 1, of which waited for: 4 -> 1; matrix products, arithmetic and copies ran while one was open for 4% -> 0% of each run, Pallas kernels for 0% -> 0%
where the time goes in v1:
time: 501 us
  Pallas kernels  363 us (72%)
  waiting for transfers between devices  58.8 us (12%)
  matrix products  54.2 us (11%)
  between operations  13.5 us (3%)
  local copies, waits for them, and re-layouts  9.28 us (2%)
    pallas_call x2, Pallas kernels, gather(): pl.pallas_call(functools.partial(gather_kernel, n, pieces, len(blocks)),...  363 us
    reduce_scatter x1, waiting for transfers between devices, per_device(): lax.psum_scatter(partial_value.astype(jnp.bfloat16), 'head', scatter_dime...  58.8 us
    dot_general x1, matrix products, per_device(): proj = jnp.einsum('td,cde->cte', tokens, w_all, preferred_element_type=f32)  25 us
    dot_general x1, matrix products, per_device(): jnp.einsum('hts,shj->thj', scores, value, preferred_element_type=f32)  10.9 us
  transfers between devices with their start and end apart: 1, of which 1 were waited for; matrix products, arithmetic and copies ran while one was open for 0% of the time, Pallas kernels for 0%

profile of v1, /device:TPU:0, one launch (start us, length us, event | category | flops | bytes accessed | tf_op | source)
XLA Modules:
  0.0 500.5 jit_solution(3546921230328351732)
XLA Ops:
  6.5 0.0 reduce-scatter.2.cloned.1.call-start
  6.5 336.1 %shard_map.55 = (bf16[3,4096,1024]{2,1,0:T(8,128)(2,1)}, bf16[1024,4096]{1,0:T(8,128)(2,1)}) custom-call(bf16[3,512,1024]{2,1,0:T(8,128)(2,1)} %refs_0_.1, bf16[1024,512]{1,0:T(8,128)(2,1)} %refs_1_.1), custom_call_target="tpu_custom_call" | custom-call | tf_op jit(solution)/shard_map/pallas_call | solution.py:131
  342.6 25.0 %fusion.7 = f32[3,768,1024]{1,2,0:T(8,128)S(1)} fusion(bf16[3,4096,1024]{2,1,0:T(8,128)(2,1)} %get-tuple-element.7, bf16[768,4096]{1,0:T(8,128)(2,1)} %param.5), kind=kOutput, calls=%fused_computation.9 | convolution fusion | flops 19327352832 | bytes 40894464 | tf_op jit(solution)/shard_map/td,cde->cte/dot_general | solution.py:200
  367.6 2.1 fusion.15
  369.7 1.3 slice.17
  371.0 1.0 iota_compare_fusion
  372.0 3.6 copy.10
  375.6 2.3 copy.8
  377.9 0.0 copy-start.1
  377.9 4.2 convolution_convert_fusion.1.refs_0_
  382.1 26.8 %shard_map.56 = bf16[8,8,128,128]{3,2,1,0:T(8,128)(2,1)} custom-call(bf16[8,128,128]{2,1,0:T(8,128)(2,1)} %convolution_convert_fusion.1.refs_0_), custom_call_target="tpu_custom_call" | custom-call | tf_op jit(solution)/shard_map/pallas_call | solution.py:131
  408.9 0.0 copy-done.1
  408.9 0.0 copy-start
  408.9 0.0 copy-start.3
  408.9 10.9 %fusion = f32[8,128,768]{2,1,0:T(8,128)} fusion(bf16[768,8,128]{0,2,1:T(8,128)(2,1)} %bitcast.29, pred[768,768]{1,0:T(8,128)(4,1)S(1)} %copy-done.1, f32[768,8,128]{2,0,1:T(8,128)} %copy.8, f32[768,8,128]{2,0,1:T(8,128)} %copy.10), kind=kOutput, calls=%fused_computation.1 | convolution fusion | flops 2433220608 | bytes 11599872 | tf_op jit(solution)/shard_map/hts,shj->thj/dot_general | solution.py:215
  419.8 0.0 copy-done
  419.8 0.0 slice-start
  419.8 0.5 select_reduce_fusion
  420.3 0.0 copy-done.3
  420.3 0.0 copy-start.2
  420.3 0.0 slice-start.1
  420.3 5.4 %fusion.10 = (f32[768,8]{0,1:T(8,128)S(1)}, f32[8,128,768]{2,1,0:T(8,128)S(1)}) fusion(f32[8,128,768]{2,1,0:T(8,128)} %fusion, f32[768,8,128]{2,0,1:T(8,128)} %copy.8, f32[8,128,128]{2,1,0:T(8,128)S(1)} %copy-done.3, f32[8,128,128]{2,1,0:T(8,128)S(1)} %select_reduce_fusion), kind=kOutput, calls=%fused_computation.13 | convolution fusion | flops 1214375936 | bytes 10510336 | tf_op jit(solution)/shard_map/thi,hij->thj/dot_general | solution.py:216
  425.7 0.0 copy-done.2
  425.8 0.4 fusion.12
  426.1 0.0 slice-done
  426.1 0.0 slice-done.1
  426.2 8.7 %convolution_convert_fusion = bf16[768,4096]{1,0:T(8,128)(2,1)} fusion(bf16[768,1024]{0,1:T(8,128)(2,1)S(1)} %bitcast.30, bf16[1024,4096]{1,0:T(8,128)(2,1)S(1)} %bitcast.33), kind=kOutput, calls=%fused_computation.4 | convolution fusion | flops 6445596672 | bytes 16252928 | tf_op jit(solution)/shard_map/dot_general | solution.py:224
  434.9 0.0 reduce-scatter.2.cloned.1.call-update
  434.9 58.8 %reduce-scatter.2.cloned.1.call-done = bf16[768,1024]{1,0:T(8,128)(2,1)} async-done(((bf16[768,4096]{1,0:T(8,128)(2,1)}), bf16[768,1024]{1,0:T(8,128)(2,1)}) %reduce-scatter.2.cloned.1.call-update) | async-done | bytes 1572880 | tf_op jit(solution)/shard_map/reduce_scatter | solution.py:225
  (3 shorter events, 0.0 us)
Async XLA Ops:
  6.5 487.2 %reduce-scatter.2.cloned.1.call-start = ((), (), s32[]{:S(2)}) async-start(), calls=%async_computation.1 | async-start | bytes 7864320 | tf_op jit(solution)/shard_map/reduce_scatter | solution.py:225
  377.9 30.9 %copy-start.1 = (pred[768,768]{1,0:T(8,128)(4,1)S(1)}, pred[768,768]{1,0:T(8,128)(4,1)}, u32[]{:S(2)}) copy-start(pred[768,768]{1,0:T(8,128)(4,1)} %iota_compare_fusion) | copy-start | bytes 1769476
  408.9 10.9 %copy-start = (bf16[8,8,128,128]{3,2,1,0:T(8,128)(2,1)S(1)}, bf16[8,8,128,128]{3,2,1,0:T(8,128)(2,1)}, u32[]{:S(2)}) copy-start(bf16[8,8,128,128]{3,2,1,0:T(8,128)(2,1)} %shard_map.56) | copy-start | bytes 6291460
  408.9 11.4 %copy-start.3 = (f32[8,128,128]{2,1,0:T(8,128)S(1)}, f32[8,128,128]{2,1,0:T(8,128)}, u32[]{:S(2)}) copy-start(f32[8,128,128]{2,1,0:T(8,128)} %param.8) | copy-start | bytes 1572868
  419.8 6.4 %slice-start = ((s8[8388608]{0:T(1024)(128)(4,1)}), s8[4194304]{0:T(1024)(128)(4,1)S(1)}, s32[]{:S(2)}) async-start(s8[8388608]{0:T(1024)(128)(4,1)} %bitcast.32), calls=%async_computation.2 | async-start | bytes 8388608
  420.3 5.5 %copy-start.2 = (f32[1024]{0:T(1024)S(1)}, f32[1024]{0:T(1024)}, u32[]{:S(2)}) copy-start(f32[1024]{0:T(1024)} %param.9) | copy-start | bytes 12292
  420.3 5.9 %slice-start.1 = ((s8[8388608]{0:T(1024)(128)(4,1)}), s8[4194304]{0:T(1024)(128)(4,1)S(1)}, s32[]{:S(2)}) async-start(s8[8388608]{0:T(1024)(128)(4,1)} %bitcast.32), calls=%async_computation.3 | async-start | bytes 8388608
Sparse Core Ops, SparseCore 0:
  435.0 58.5 reduce-scatter.1

commit v2 on v1

--- a/solution.py
+++ b/solution.py
@@ -142,11 +142,10 @@
     )(*blocks)
 
 
-def gather_weights(w_qkv, w_out):
+def gather_weights(w_qkv):
     n = lax.axis_size("seq")
     _, depth, cols = w_qkv.shape
-    rows, width = w_out.shape
-    half, quarter = depth // 2, rows // 4
+    half = depth // 2
     pieces = []
 
     def rows_piece(c, part, cross):
@@ -157,22 +156,10 @@
             cross,
         ))
 
-    def cols_piece(part, cross):
-        span = pl.ds(part * quarter, quarter)
-        pieces.append((
-            1,
-            (span,),
-            lambda owner: (span, pl.ds(pl.multiple_of(owner * width, width), width)),
-            cross,
-        ))
-
     for c in range(3):
         for part in range(2):
             rows_piece(c, part, c == 0 and part == 0)
-    for part in range(4):
-        cols_piece(part, part == 0)
-    shapes = ((3, n * depth, cols), (rows, n * width))
-    return gather(n, 0, pieces, shapes, w_qkv, w_out)
+    return gather(n, 0, pieces, ((3, n * depth, cols),), w_qkv)[0]
 
 
 def gather_states(states):
@@ -191,12 +178,122 @@
     return gather(n, 1, pieces, ((n, *states.shape),), states)[0]
 
 
+def project_kernel(n, part, normed_ref, w_ref, out_ref, core_out, core_in, far_out, far_in, *sems):
+    core_send, core_recv, far_send, far_recv = sems
+    chips = n // 2
+    width = w_ref.shape[1] // n
+    parts = width // part
+    me = lax.axis_index("head")
+    chip, core = me // 2, me % 2
+    buddy = chip * 2 + 1 - core
+
+    def there(turn):
+        return lax.rem(chip + turn, chips)
+
+    barrier = pltpu.get_barrier_semaphore()
+    for peer in [buddy] + [there(turn) * 2 + core for turn in range(1, chips)]:
+        pl.semaphore_signal(barrier, inc=1, device_id={"head": peer}, device_id_type=MESH)
+    pl.semaphore_wait(barrier, chips)
+
+    def product(group, p):
+        columns = pl.ds(pl.multiple_of(group * width + p * part, part), part)
+        return jnp.dot(normed_ref[...], w_ref[:, columns], preferred_element_type=jnp.float32)
+
+    def to_core(turn, p):
+        return pltpu.make_async_remote_copy(
+            src_ref=core_out.at[turn, p],
+            dst_ref=core_in.at[turn, p],
+            send_sem=core_send.at[turn, p],
+            recv_sem=core_recv.at[turn, p],
+            device_id={"head": buddy},
+            device_id_type=MESH,
+        )
+
+    def to_chip(turn, p):
+        return pltpu.make_async_remote_copy(
+            src_ref=far_out.at[turn - 1, p],
+            dst_ref=far_in.at[turn - 1, p],
+            send_sem=far_send.at[turn - 1, p],
+            recv_sem=far_recv.at[turn - 1, p],
+            device_id={"head": there(turn) * 2 + core},
+            device_id_type=MESH,
+        )
+
+    for turn in [*range(1, chips), 0]:
+
+        @pl.loop(0, parts)
+        def _(p):
+            core_out[turn, p] = product(there(turn) * 2 + 1 - core, p).astype(core_out.dtype)
+            to_core(turn, p).start()
+
+        @pl.loop(0, parts)
+        def _(p):
+            total = product(there(turn) * 2 + core, p)
+            to_core(turn, p).wait_recv()
+            total += core_in[turn, p].astype(jnp.float32)
+            if turn:
+                far_out[turn - 1, p] = total.astype(far_out.dtype)
+                to_chip(turn, p).start()
+            else:
+                for other in range(1, chips):
+                    to_chip(other, p).wait_recv()
+                    total += far_in[other - 1, p].astype(jnp.float32)
+                out_ref[:, pl.ds(pl.multiple_of(p * part, part), part)] = total.astype(out_ref.dtype)
+
+    for turn in range(chips):
+
+        @pl.loop(0, parts)
+        def _(p):
+            to_core(turn, p).wait_send()
+            if turn:
+                to_chip(turn, p).wait_send()
+
+
+def project_and_sum(normed, w_out):
+    n = lax.axis_size("head")
+    rows, depth = normed.shape
+    columns = w_out.shape[1]
+    width = columns // n
+    part = min(width, 256)
+    chips, parts = n // 2, width // part
+    near = pltpu.VMEM((chips, parts, rows, part), jnp.bfloat16)
+    far = pltpu.VMEM((chips - 1, parts, rows, part), jnp.bfloat16)
+    dma = pltpu.SemaphoreType.DMA
+    inside = pl.BlockSpec(memory_space=pltpu.VMEM)
+    return pl.pallas_call(
+        functools.partial(project_kernel, n, part),
+        out_shape=jax.ShapeDtypeStruct((rows, width), jnp.bfloat16),
+        in_specs=[inside, inside],
+        out_specs=inside,
+        scratch_shapes=[
+            near,
+            near,
+            far,
+            far,
+            dma((chips, parts)),
+            dma((chips, parts)),
+            dma((chips - 1, parts)),
+            dma((chips - 1, parts)),
+        ],
+        compiler_params=pltpu.CompilerParams(
+            collective_id=2, has_side_effects=True, vmem_limit_bytes=48 * 2**20
+        ),
+        cost_estimate=pl.CostEstimate(
+            flops=2 * rows * depth * columns,
+            bytes_accessed=2 * (rows * depth + depth * columns + rows * width),
+            transcendentals=0,
+        ),
+    )(normed, w_out)
+
+
 def per_device(tokens, w_qkv, w_out, prior_state, norm_gain):
     f32 = jnp.float32
     rows = tokens.shape[0]
     cols = w_qkv.shape[2]
     heads = cols // HEAD_DIM
-    w_all, w_out_all = gather_weights(w_qkv, w_out)
+    w_all = gather_weights(w_qkv)
+    w_all, w_out = lax.optimization_barrier((w_all, w_out))
+    w_out_all = lax.all_gather(w_out, "seq", axis=1, tiled=True)
     proj = jnp.einsum("td,cde->cte", tokens, w_all, preferred_element_type=f32)
     query = jax.nn.silu(proj[0]).astype(jnp.bfloat16).reshape(rows, heads, HEAD_DIM)
     key = jax.nn.silu(proj[1]).astype(jnp.bfloat16).reshape(rows, heads, HEAD_DIM)
@@ -221,10 +318,7 @@
         .astype(jnp.bfloat16)
         .reshape(rows, cols)
     )
-    partial_value = jnp.dot(normed, w_out_all, preferred_element_type=f32)
-    return lax.psum_scatter(
-        partial_value.astype(jnp.bfloat16), "head", scatter_dimension=1, tiled=True
-    )
+    return project_and_sum(normed, w_out_all)
 
 
 def solution(mesh):

time: 501 us -> 465 us (0.928)
  waiting for transfers between devices: 58.8 us -> 22.8 us
  matrix products: 54.2 us -> 43.5 us
  Pallas kernels: 363 us -> 369 us
    reduce_scatter x1 -> x0, waiting for transfers between devices: 58.8 us -> none  [per_device(): lax.psum_scatter(partial_value.astype(jnp.bfloat16), 'head', scatter_dime...]
    pallas_call x0 -> x1, Pallas kernels: none -> 43.4 us  [project_and_sum(): pl.pallas_call(functools.partial(project_kernel, n, part), out_shape=jax....]
    pallas_call x2, Pallas kernels: 363 us -> 326 us  [gather(): pl.pallas_call(functools.partial(gather_kernel, n, pieces, len(blocks)),...]
    all_gather x0 -> x1, waiting for transfers between devices: none -> 22.8 us  [per_device(): w_out_all = lax.all_gather(w_out, 'seq', axis=1, tiled=True)]
    dot_general x1 -> x0, matrix products: 8.74 us -> none  [per_device(): partial_value = jnp.dot(normed, w_out_all, preferred_element_type=f32)]
  transfers between devices with their start and end apart: 1 -> 1, of which waited for: 1 -> 1; matrix products, arithmetic and copies ran while one was open for 0% -> 12% of each run, Pallas kernels for 0% -> 15%
where the time goes in v2:
time: 465 us; the launch traced here: 464 us
  Pallas kernels  369 us (79%)
  matrix products  43.5 us (9%)
  waiting for transfers between devices  22.8 us (5%)
  between operations  13.5 us (3%)
  local copies, waits for them, and re-layouts  11.2 us (2%)
    pallas_call x2, Pallas kernels, gather(): pl.pallas_call(functools.partial(gather_kernel, n, pieces, len(blocks)),...  326 us
    pallas_call x1, Pallas kernels, project_and_sum(): pl.pallas_call(functools.partial(project_kernel, n, part), out_shape=jax....  43.4 us
    dot_general x1, matrix products, per_device(): proj = jnp.einsum('td,cde->cte', tokens, w_all, preferred_element_type=f32)  25 us
    all_gather x1, waiting for transfers between devices, per_device(): w_out_all = lax.all_gather(w_out, 'seq', axis=1, tiled=True)  22.8 us
    dot_general x1, matrix products, per_device(): jnp.einsum('hts,shj->thj', scores, value, preferred_element_type=f32)  9.9 us
  transfers between devices with their start and end apart: 1, of which 1 were waited for; matrix products, arithmetic and copies ran while one was open for 12% of the time, Pallas kernels for 15%

profile of v2, /device:TPU:0, one launch (start us, length us, event | category | flops | bytes accessed | tf_op | source)
XLA Modules:
  0.0 464.4 jit_solution(18191349200089284553)
XLA Ops:
  6.5 0.0 all-gather.2.cloned.1.call-start
  6.5 256.1 %shard_map.55 = bf16[3,4096,1024]{2,1,0:T(8,128)(2,1)} custom-call(bf16[3,512,1024]{2,1,0:T(8,128)(2,1)} %refs_0_.1), custom_call_target="tpu_custom_call" | custom-call | tf_op jit(solution)/shard_map/pallas_call | solution.py:131
  262.6 0.0 all-gather.2.cloned.1.call-update
  262.7 25.0 %fusion.7 = f32[3,768,1024]{1,2,0:T(8,128)S(1)} fusion(bf16[3,4096,1024]{2,1,0:T(8,128)(2,1)} %shard_map.55, bf16[768,4096]{1,0:T(8,128)(2,1)} %param.5), kind=kOutput, calls=%fused_computation.8 | convolution fusion | flops 19327352832 | bytes 40894464 | tf_op jit(solution)/shard_map/td,cde->cte/dot_general | solution.py:297
  287.7 1.3 slice.17
  289.0 2.1 fusion.15
  291.1 3.5 copy.10
  294.6 2.4 copy.8
  297.0 4.1 convolution_convert_fusion.refs_0_
  301.1 0.0 copy-start
  301.1 69.5 %shard_map.56 = bf16[8,8,128,128]{3,2,1,0:T(8,128)(2,1)} custom-call(bf16[8,128,128]{2,1,0:T(8,128)(2,1)} %convolution_convert_fusion.refs_0_), custom_call_target="tpu_custom_call" | custom-call | tf_op jit(solution)/shard_map/pallas_call | solution.py:131
  370.6 1.0 iota_compare_fusion
  371.7 3.0 select_reduce_fusion
  374.7 0.0 copy-done
  374.7 9.9 %fusion = f32[8,128,768]{2,1,0:T(8,128)} fusion(bf16[768,8,128]{0,2,1:T(8,128)(2,1)} %bitcast.28, pred[768,768]{1,0:T(8,128)(4,1)} %iota_compare_fusion, f32[768,8,128]{2,0,1:T(8,128)S(1)} %copy-done, f32[768,8,128]{2,0,1:T(8,128)} %copy.10), kind=kOutput, calls=%fused_computation.1 | convolution fusion | flops 2433220608 | bytes 11599872 | tf_op jit(solution)/shard_map/hts,shj->thj/dot_general | solution.py:312
  384.6 0.0 copy-start.1
  384.6 4.5 fusion.10
  389.1 0.0 copy-done.1
  389.1 0.4 fusion.12
  389.5 0.8 copy.15.normed_ref
  390.3 22.8 %all-gather.2.cloned.1.call-done.w_ref = bf16[1024,4096]{1,0:T(8,128)(2,1)} async-done(((bf16[1024,512]{1,0:T(8,128)(2,1)}), bf16[1024,4096]{1,0:T(8,128)(2,1)}) %all-gather.2.cloned.1.call-update) | async-done | bytes 8388624 | tf_op jit(solution)/shard_map/all_gather | solution.py:296
  413.1 43.4 %shard_map.57 = bf16[768,1024]{1,0:T(8,128)(2,1)S(1)} custom-call(bf16[768,1024]{1,0:T(8,128)(2,1)S(1)} %copy.15.normed_ref, bf16[1024,4096]{1,0:T(8,128)(2,1)} %all-gather.2.cloned.1.call-done.w_ref), custom_call_target="tpu_custom_call" | custom-call | flops 6442450944 | bytes 11534336 | tf_op jit(solution)/shard_map/pallas_call | solution.py:263
  456.4 1.1 copy.17
  (2 shorter events, 0.0 us)
Async XLA Ops:
  6.5 406.5 %all-gather.2.cloned.1.call-start = ((), (), s32[]{:S(2)}) async-start(), calls=%async_computation | async-start | bytes 9437184 | tf_op jit(solution)/shard_map/all_gather | solution.py:296
  301.1 73.5 %copy-start = (f32[768,8,128]{2,0,1:T(8,128)S(1)}, f32[768,8,128]{2,0,1:T(8,128)}, u32[]{:S(2)}) copy-start(f32[768,8,128]{2,0,1:T(8,128)} %copy.8) | copy-start | bytes 9437188
  384.6 4.6 copy-start.1
Sparse Core Ops, SparseCore 0:
  262.8 150.2 all-gather.1

commit v3 on v2

--- a/solution.py
+++ b/solution.py
@@ -12,8 +12,37 @@
 
 
 def gather_kernel(n, pieces, arrays, *refs):
-    ins, outs = refs[:arrays], refs[arrays : 2 * arrays]
-    send_sem, recv_sem, local_sem = refs[2 * arrays :]
+    relay(n, pieces, refs[:arrays], refs[arrays : 2 * arrays], *refs[2 * arrays :])
+
+
+def weights_kernel(n, pieces, depth, tokens_ref, w_ref, w_out_ref, proj_ref, w_out_all, w_all, total, *sems):
+    width = 256
+
+    def visit(owner, first=False):
+        columns = pl.ds(pl.multiple_of(owner * depth, depth), depth)
+        for c in range(3):
+
+            @pl.loop(0, w_all.shape[2] // width)
+            def _(tile):
+                span = pl.ds(pl.multiple_of(tile * width, width), width)
+                new = jnp.dot(
+                    tokens_ref[:, columns], w_all[c, columns, span], preferred_element_type=jnp.float32
+                )
+                total[c, :, span] = new if first else total[c, :, span] + new
+
+    relay(n, pieces, (w_ref, w_out_ref), (w_all, w_out_all), *sems, visit=visit)
+    for c in range(3):
+
+        @pl.loop(0, w_all.shape[2] // width)
+        def _(tile):
+            span = pl.ds(pl.multiple_of(tile * width, width), width)
+            value = total[c, :, span]
+            if c < 2:
+                value = value / (1.0 + jnp.exp(-value))
+            proj_ref[c, :, span] = value.astype(proj_ref.dtype)
+
+
+def relay(n, pieces, ins, outs, send_sem, recv_sem, local_sem, visit=None):
     me = lax.axis_index("seq")
     length = n // 2
     row, side = me // 2, me % 2
@@ -102,22 +131,55 @@
     begin(lambda c: c.start())
     for c in locals_:
         c.start()
+    if visit:
+        for c in locals_:
+            c.wait()
+        visit(me, True)
     crossed(True, lambda c: c.start())
+
+    def beyond(owner):
+        for array in range(len(ins)):
+            for piece, (which, _, _, cross) in enumerate(pieces):
+                if which == array and not cross:
+                    copy(owner, piece, 2).wait_recv()
+            if visit and array == 0:
+                visit(owner)
+
+    def either(step, act):
+        @pl.when(row >= step)
+        def _():
+            act(row - step)
+
+        @pl.when(row + step < length)
+        def _():
+            act(row + step)
 
     @pl.loop(1, length)
     def _(step):
         along(step, True, lambda c: c.start())
-
-    @pl.loop(0, length)
-    def _(other):
-        owner = other * 2 + 1 - side
-        for piece, (_, _, _, cross) in enumerate(pieces):
-            if not cross:
-                copy(owner, piece, 2).wait_recv()
+        if visit:
+            either(step, lambda r: visit(r * 2 + side))
+
+            @pl.when(step == 1)
+            def _():
+                beyond(pair)
+
+            @pl.when(step > 1)
+            def _():
+                either(step - 1, lambda r: beyond(r * 2 + 1 - side))
+
+    if visit:
+        either(length - 1, lambda r: beyond(r * 2 + 1 - side))
+    else:
+
+        @pl.loop(0, length)
+        def _(other):
+            beyond(other * 2 + 1 - side)
 
     begin(lambda c: c.wait_send())
-    for c in locals_:
-        c.wait()
+    if not visit:
+        for c in locals_:
+            c.wait()
     crossed(False, lambda c: c.wait_send())
 
     @pl.loop(1, length)
@@ -142,10 +204,11 @@
     )(*blocks)
 
 
-def gather_weights(w_qkv):
+def project_in(tokens, w_qkv, w_out):
     n = lax.axis_size("seq")
     _, depth, cols = w_qkv.shape
-    half = depth // 2
+    rows, width = w_out.shape
+    half, band = depth // 2, rows // 6
     pieces = []
 
     def rows_piece(c, part, cross):
@@ -156,10 +219,42 @@
             cross,
         ))
 
+    def cols_piece(part, cross):
+        span = pl.ds(part * band, band)
+        pieces.append((
+            1,
+            (span,),
+            lambda owner: (span, pl.ds(pl.multiple_of(owner * width, width), width)),
+            cross,
+        ))
+
     for c in range(3):
         for part in range(2):
             rows_piece(c, part, c == 0 and part == 0)
-    return gather(n, 0, pieces, ((3, n * depth, cols),), w_qkv)[0]
+    for part in range(6):
+        cols_piece(part, part == 0)
+    count = len(pieces)
+    anywhere = pl.BlockSpec(memory_space=pl.ANY)
+    inside = pl.BlockSpec(memory_space=pltpu.VMEM)
+    return pl.pallas_call(
+        functools.partial(weights_kernel, n, pieces, depth),
+        out_shape=[
+            jax.ShapeDtypeStruct((3, tokens.shape[0], cols), jnp.bfloat16),
+            jax.ShapeDtypeStruct((rows, n * width), jnp.bfloat16),
+        ],
+        in_specs=[inside, anywhere, anywhere],
+        out_specs=[inside, anywhere],
+        scratch_shapes=[
+            pltpu.VMEM((3, n * depth, cols), jnp.bfloat16),
+            pltpu.VMEM((3, tokens.shape[0], cols), jnp.float32),
+            pltpu.SemaphoreType.DMA((3, n, count)),
+            pltpu.SemaphoreType.DMA((n, count)),
+            pltpu.SemaphoreType.DMA((count,)),
+        ],
+        compiler_params=pltpu.CompilerParams(
+            collective_id=0, has_side_effects=True, vmem_limit_bytes=54 * 2**20
+        ),
+    )(tokens, w_qkv, w_out)
 
 
 def gather_states(states):
@@ -178,7 +273,7 @@
     return gather(n, 1, pieces, ((n, *states.shape),), states)[0]
 
 
-def project_kernel(n, part, normed_ref, w_ref, out_ref, core_out, core_in, far_out, far_in, *sems):
+def project_kernel(n, part, normed_ref, w_ref, late_ref, out_ref, core_out, core_in, far_out, far_in, *sems):
     core_send, core_recv, far_send, far_recv = sems
     chips = n // 2
     width = w_ref.shape[1] // n
@@ -197,7 +292,10 @@
 
     def product(group, p):
         columns = pl.ds(pl.multiple_of(group * width + p * part, part), part)
-        return jnp.dot(normed_ref[...], w_ref[:, columns], preferred_element_type=jnp.float32)
+        early = w_ref.shape[0]
+        return jnp.dot(
+            normed_ref[:, :early], w_ref[:, columns], preferred_element_type=jnp.float32
+        ) + jnp.dot(normed_ref[:, early:], late_ref[:, columns], preferred_element_type=jnp.float32)
 
     def to_core(turn, p):
         return pltpu.make_async_remote_copy(
@@ -249,10 +347,10 @@
                 to_chip(turn, p).wait_send()
 
 
-def project_and_sum(normed, w_out):
+def project_and_sum(normed, w_early, w_late):
     n = lax.axis_size("head")
     rows, depth = normed.shape
-    columns = w_out.shape[1]
+    columns = w_early.shape[1]
     width = columns // n
     part = min(width, 256)
     chips, parts = n // 2, width // part
@@ -263,7 +361,7 @@
     return pl.pallas_call(
         functools.partial(project_kernel, n, part),
         out_shape=jax.ShapeDtypeStruct((rows, width), jnp.bfloat16),
-        in_specs=[inside, inside],
+        in_specs=[inside, inside, inside],
         out_specs=inside,
         scratch_shapes=[
             near,
@@ -283,7 +381,7 @@
             bytes_accessed=2 * (rows * depth + depth * columns + rows * width),
             transcendentals=0,
         ),
-    )(normed, w_out)
+    )(normed, w_early, w_late)
 
 
 def per_device(tokens, w_qkv, w_out, prior_state, norm_gain):
@@ -291,13 +389,11 @@
     rows = tokens.shape[0]
     cols = w_qkv.shape[2]
     heads = cols // HEAD_DIM
-    w_all = gather_weights(w_qkv)
-    w_all, w_out = lax.optimization_barrier((w_all, w_out))
-    w_out_all = lax.all_gather(w_out, "seq", axis=1, tiled=True)
-    proj = jnp.einsum("td,cde->cte", tokens, w_all, preferred_element_type=f32)
-    query = jax.nn.silu(proj[0]).astype(jnp.bfloat16).reshape(rows, heads, HEAD_DIM)
-    key = jax.nn.silu(proj[1]).astype(jnp.bfloat16).reshape(rows, heads, HEAD_DIM)
-    value = proj[2].astype(jnp.bfloat16).reshape(rows, heads, HEAD_DIM)
+    early = w_out.shape[0] * 3 // 4
+    proj, w_early = project_in(tokens, w_qkv, w_out[:early])
+    proj, w_late = lax.optimization_barrier((proj, w_out[early:]))
+    w_late = lax.all_gather(w_late, "seq", axis=1, tiled=True)
+    query, key, value = (proj[c].reshape(rows, heads, HEAD_DIM) for c in range(3))
     local = jnp.einsum("thi,thj->hij", key, value, preferred_element_type=f32)
     states = gather_states(local.astype(jnp.bfloat16))
     before = jnp.arange(states.shape[0]) < lax.axis_index("seq")
@@ -318,7 +414,7 @@
         .astype(jnp.bfloat16)
         .reshape(rows, cols)
     )
-    return project_and_sum(normed, w_out_all)
+    return project_and_sum(normed, w_early, w_late)
 
 
 def solution(mesh):

time: 465 us -> 462 us (level)
  Pallas kernels: 369 us -> 414 us
  matrix products: 43.5 us -> 14.4 us
  waiting for transfers between devices: 22.8 us -> 0.04 us
  local copies, waits for them, and re-layouts: 11.2 us -> 16.9 us
    pallas_call x0 -> x1, Pallas kernels: none -> 325 us  [project_in(): pl.pallas_call(functools.partial(weights_kernel, n, pieces, depth), out_s...]
    pallas_call x2 -> x1, Pallas kernels: 326 us -> 46.3 us  [gather(): pl.pallas_call(functools.partial(gather_kernel, n, pieces, len(blocks)),...]
    dot_general x1 -> x0, matrix products: 25 us -> none  [per_device(): proj = jnp.einsum('td,cde->cte', tokens, w_all, preferred_element_type=f32)]
    all_gather x1, waiting for transfers between devices: 22.8 us -> 0.02 us  [per_device(): w_late = lax.all_gather(w_late, 'seq', axis=1, tiled=True)]
    unnamed x5 -> x14, local copies, waits for them, and re-layouts: 1.15 us -> 9.76 us
    squeeze x2 -> x0, local copies, waits for them, and re-layouts: 5.92 us -> none  [the longest x1 3.55 us: per_device(): proj[1]]
  transfers between devices with their start and end apart: 1 -> 1, of which waited for: 1 -> 0; matrix products, arithmetic and copies ran while one was open for 12% -> 6% of each run, Pallas kernels for 15% -> 10%
where the time goes in v3:
time: 462 us; the launch traced here: 461 us
  Pallas kernels  414 us (90%)
  local copies, waits for them, and re-layouts  16.9 us (4%)
  matrix products  14.4 us (3%)
  between operations  13.5 us (3%)
    pallas_call x1, Pallas kernels, project_in(): pl.pallas_call(functools.partial(weights_kernel, n, pieces, depth), out_s...  325 us
    pallas_call x1, Pallas kernels, gather(): pl.pallas_call(functools.partial(gather_kernel, n, pieces, len(blocks)),...  46.3 us
    pallas_call x1, Pallas kernels, project_and_sum(): pl.pallas_call(functools.partial(project_kernel, n, part), out_shape=jax....  42.7 us
    unnamed x14, local copies, waits for them, and re-layouts  9.76 us
    dot_general x1, matrix products, per_device(): jnp.einsum('hts,shj->thj', scores, value, preferred_element_type=f32)  9.38 us
  transfers between devices with their start and end apart: 1, of which 0 were waited for; matrix products, arithmetic and copies ran while one was open for 6% of the time, Pallas kernels for 10%

profile of v3, /device:TPU:0, one launch (start us, length us, event | category | flops | bytes accessed | tf_op | source)
XLA Modules:
  0.0 461.4 jit_solution(996758258413195360)
XLA Ops:
  6.5 0.0 all-gather.2.cloned.1.call-start
  6.5 2.1 slice.15.w_out_ref
  8.6 1.7 slice.16
  10.3 324.9 %shard_map.55 = (bf16[3,768,1024]{2,1,0:T(8,128)(2,1)}, bf16[768,4096]{1,0:T(8,128)(2,1)}) custom-call(bf16[768,4096]{1,0:T(8,128)(2,1)} %tokens_ref.1, bf16[3,512,1024]{2,1,0:T(8,128)(2,1)} %w_ref.1, bf16[768,512]{1,0:T(8,128)(2,1)} %slice.15.w_out_ref), custom_call_target="tpu_custom_call" | custom-call | tf_op jit(solution)/shard_map/pallas_call | solution.py:239
  335.2 0.0 all-gather.2.cloned.1.call-update
  335.3 4.6 slice_bitcast_fusion
  339.8 2.6 copy.13
  342.4 0.4 copy.15
  342.9 0.0 copy-start.2
  342.9 0.0 copy-start.1
  342.9 0.4 copy.16
  343.4 0.7 copy-done.2
  344.0 0.9 copy-done.1
  344.9 1.3 fusion.14.refs_0_
  346.3 46.3 %shard_map.56 = bf16[8,8,128,128]{3,2,1,0:T(8,128)(2,1)} custom-call(bf16[8,128,128]{2,1,0:T(8,128)(2,1)} %fusion.14.refs_0_), custom_call_target="tpu_custom_call" | custom-call | tf_op jit(solution)/shard_map/pallas_call | solution.py:193
  392.6 0.2 iota_compare_fusion
  392.7 2.1 select_reduce_fusion
  394.9 0.0 copy-start.3
  394.9 9.4 %fusion = f32[8,128,768]{2,1,0:T(8,128)} fusion(pred[768,768]{1,0:T(8,128)(4,1)S(1)} %iota_compare_fusion, bf16[768,8,128]{0,2,1:T(8,128)(2,1)} %bitcast.25, bf16[768,8,128]{2,1,0:T(8,128)(2,1)} %bitcast.28, bf16[768,8,128]{2,1,0:T(8,128)(2,1)S(1)} %bitcast.22), kind=kOutput, calls=%fused_computation.1 | convolution fusion | flops 2425356288 | bytes 8454144 | tf_op jit(solution)/shard_map/hts,shj->thj/dot_general | solution.py:408
  404.3 0.0 copy-done.3
  404.3 0.0 copy-start.4
  404.3 3.7 fusion.5
  407.9 0.0 copy-done.4
  408.0 0.4 fusion.7
  408.3 0.8 copy.14.normed_ref
  409.1 0.0 all-gather.2.cloned.1.call-done.late_ref
  409.1 0.0 copy-start
  409.1 1.6 copy-done
  410.7 42.7 %shard_map.57 = bf16[768,1024]{1,0:T(8,128)(2,1)S(1)} custom-call(bf16[768,1024]{1,0:T(8,128)(2,1)S(1)} %copy.14.normed_ref, bf16[768,4096]{1,0:T(8,128)(2,1)} %get-tuple-element.11.w_ref, bf16[256,4096]{1,0:T(8,128)(2,1)S(1)} %copy-done), custom_call_target="tpu_custom_call" | custom-call | flops 6442450944 | bytes 11534336 | tf_op jit(solution)/shard_map/pallas_call | solution.py:361
  453.4 1.1 copy.31
  (2 shorter events, 0.0 us)
Async XLA Ops:
  6.5 402.6 %all-gather.2.cloned.1.call-start = ((), (), s32[]{:S(2)}) async-start(), calls=%async_computation | async-start | bytes 2359296 | tf_op jit(solution)/shard_map/all_gather | solution.py:395
  342.9 1.1 copy-start.2
  342.9 2.0 copy-start.1
  394.9 9.4 %copy-start.3 = (f32[8,128,128]{2,1,0:T(8,128)S(1)}, f32[8,128,128]{2,1,0:T(8,128)}, u32[]{:S(2)}) copy-start(f32[8,128,128]{2,1,0:T(8,128)} %param.8) | copy-start | bytes 1572868
  404.3 3.7 copy-start.4
  409.1 1.6 copy-start
Sparse Core Ops, SparseCore 0:
  335.4 61.3 all-gather.1

commit v4 on v3

--- a/solution.py
+++ b/solution.py
@@ -15,7 +15,7 @@
     relay(n, pieces, refs[:arrays], refs[arrays : 2 * arrays], *refs[2 * arrays :])
 
 
-def weights_kernel(n, pieces, depth, tokens_ref, w_ref, w_out_ref, proj_ref, w_out_all, w_all, total, *sems):
+def weights_kernel(n, pieces, depth, tokens_ref, w_ref, w_out_ref, query_ref, key_ref, value_ref, w_out_all, w_all, total, *sems):
     width = 256
 
     def visit(owner, first=False):
@@ -39,7 +39,10 @@
             value = total[c, :, span]
             if c < 2:
                 value = value / (1.0 + jnp.exp(-value))
-            proj_ref[c, :, span] = value.astype(proj_ref.dtype)
+            for part in range(width // HEAD_DIM):
+                block = value[:, part * HEAD_DIM : (part + 1) * HEAD_DIM]
+                head = tile * (width // HEAD_DIM) + part
+                (query_ref, key_ref, value_ref)[c][head] = block.astype(query_ref.dtype)
 
 
 def relay(n, pieces, ins, outs, send_sem, recv_sem, local_sem, visit=None):
@@ -204,11 +207,11 @@
     )(*blocks)
 
 
-def project_in(tokens, w_qkv, w_out):
+def project_in(tokens, w_qkv, w_out, early):
     n = lax.axis_size("seq")
     _, depth, cols = w_qkv.shape
-    rows, width = w_out.shape
-    half, band = depth // 2, rows // 6
+    width = w_out.shape[1]
+    half, band = depth // 2, early // 4
     pieces = []
 
     def rows_piece(c, part, cross):
@@ -231,7 +234,7 @@
     for c in range(3):
         for part in range(2):
             rows_piece(c, part, c == 0 and part == 0)
-    for part in range(6):
+    for part in range(4):
         cols_piece(part, part == 0)
     count = len(pieces)
     anywhere = pl.BlockSpec(memory_space=pl.ANY)
@@ -239,11 +242,11 @@
     return pl.pallas_call(
         functools.partial(weights_kernel, n, pieces, depth),
         out_shape=[
-            jax.ShapeDtypeStruct((3, tokens.shape[0], cols), jnp.bfloat16),
-            jax.ShapeDtypeStruct((rows, n * width), jnp.bfloat16),
+            *[jax.ShapeDtypeStruct((cols // HEAD_DIM, tokens.shape[0], HEAD_DIM), jnp.bfloat16)] * 3,
+            jax.ShapeDtypeStruct((early, n * width), jnp.bfloat16),
         ],
         in_specs=[inside, anywhere, anywhere],
-        out_specs=[inside, anywhere],
+        out_specs=[inside, inside, inside, anywhere],
         scratch_shapes=[
             pltpu.VMEM((3, n * depth, cols), jnp.bfloat16),
             pltpu.VMEM((3, tokens.shape[0], cols), jnp.float32),
@@ -389,29 +392,29 @@
     rows = tokens.shape[0]
     cols = w_qkv.shape[2]
     heads = cols // HEAD_DIM
-    early = w_out.shape[0] * 3 // 4
-    proj, w_early = project_in(tokens, w_qkv, w_out[:early])
-    proj, w_late = lax.optimization_barrier((proj, w_out[early:]))
+    early = w_out.shape[0] // 2
+    query, key, value, w_early = project_in(tokens, w_qkv, w_out, early)
+    query, w_late = lax.optimization_barrier((query, w_out[early:]))
     w_late = lax.all_gather(w_late, "seq", axis=1, tiled=True)
-    query, key, value = (proj[c].reshape(rows, heads, HEAD_DIM) for c in range(3))
-    local = jnp.einsum("thi,thj->hij", key, value, preferred_element_type=f32)
+    local = jnp.einsum("hti,htj->hij", key, value, preferred_element_type=f32)
     states = gather_states(local.astype(jnp.bfloat16))
     before = jnp.arange(states.shape[0]) < lax.axis_index("seq")
     earlier = jnp.sum(
         jnp.where(before[:, None, None, None], states.astype(f32), 0.0), axis=0
     )
     prefix = prior_state + earlier
-    scores = jnp.einsum("thi,shi->hts", query, key, preferred_element_type=f32)
+    scores = jnp.einsum("hti,hsi->hts", query, key, preferred_element_type=f32)
     place = jnp.arange(rows)
     keep = place[None, :] <= place[:, None]
     scores = jnp.where(keep[None], scores, 0.0).astype(jnp.bfloat16)
-    inner = jnp.einsum("hts,shj->thj", scores, value, preferred_element_type=f32)
-    outer = jnp.einsum("thi,hij->thj", query.astype(f32), prefix, precision=lax.Precision.HIGHEST)
+    inner = jnp.einsum("hts,hsj->htj", scores, value, preferred_element_type=f32)
+    outer = jnp.einsum("hti,hij->htj", query.astype(f32), prefix, precision=lax.Precision.HIGHEST)
     attended = inner + outer
     scale = lax.rsqrt(jnp.mean(attended * attended, axis=2, keepdims=True) + 1e-06)
     normed = (
-        (attended * scale * norm_gain.reshape(heads, HEAD_DIM))
+        (attended * scale * norm_gain.reshape(heads, 1, HEAD_DIM))
         .astype(jnp.bfloat16)
+        .transpose(1, 0, 2)
         .reshape(rows, cols)
     )
     return project_and_sum(normed, w_early, w_late)

time: 462 us -> 451 us (0.976)
  Pallas kernels: 414 us -> 398 us
  waiting for transfers between devices: 0.04 us -> 15.6 us
  local copies, waits for them, and re-layouts: 16.9 us -> 3.81 us
    pallas_call x1, Pallas kernels: 325 us -> 307 us  [project_in(): pl.pallas_call(functools.partial(weights_kernel, n, pieces, depth), out_s...]
    all_gather x1, waiting for transfers between devices: 0.02 us -> 15.6 us  [per_device(): w_late = lax.all_gather(w_late, 'seq', axis=1, tiled=True)]
    unnamed x14 -> x3, local copies, waits for them, and re-layouts: 9.76 us -> 1.15 us
  transfers between devices with their start and end apart: 1 -> 1, of which waited for: 0 -> 1; matrix products, arithmetic and copies ran while one was open for 6% -> 4% of each run, Pallas kernels for 10% -> 11%
where the time goes in v4:
time: 451 us
  Pallas kernels  398 us (88%)
  waiting for transfers between devices  15.6 us (3%)
  matrix products  14.8 us (3%)
  between operations  13.5 us (3%)
    pallas_call x1, Pallas kernels, project_in(): pl.pallas_call(functools.partial(weights_kernel, n, pieces, depth), out_s...  307 us
    pallas_call x1, Pallas kernels, gather(): pl.pallas_call(functools.partial(gather_kernel, n, pieces, len(blocks)),...  47.8 us
    pallas_call x1, Pallas kernels, project_and_sum(): pl.pallas_call(functools.partial(project_kernel, n, part), out_shape=jax....  43.4 us
    all_gather x1, waiting for transfers between devices, per_device(): w_late = lax.all_gather(w_late, 'seq', axis=1, tiled=True)  15.6 us
  transfers between devices with their start and end apart: 1, of which 1 were waited for; matrix products, arithmetic and copies ran while one was open for 4% of the time, Pallas kernels for 11%

profile of v4, /device:TPU:0, one launch (start us, length us, event | category | flops | bytes accessed | tf_op | source)
XLA Modules:
  0.0 450.5 jit_solution(482340279894174795)
XLA Ops:
  6.5 0.0 all-gather.2.cloned.1.call-start
  6.5 1.9 slice.3
  8.4 307.3 %shard_map.55 = (bf16[8,768,128]{2,1,0:T(8,128)(2,1)}, bf16[8,768,128]{2,1,0:T(8,128)(2,1)}, bf16[8,768,128]{2,1,0:T(8,128)(2,1)}, bf16[512,4096]{1,0:T(8,128)(2,1)}) custom-call(bf16[768,4096]{1,0:T(8,128)(2,1)} %tokens_ref.1, bf16[3,512,1024]{2,1,0:T(8,128)(2,1)} %w_ref.1, bf16[1024,512]{1,0:T(8,128)(2,1)} %w_out_ref.1), custom_call_target="tpu_custom_call" | custom-call | tf_op jit(solution)/shard_map/pallas_call | solution.py:242
  315.8 0.0 all-gather.2.cloned.1.call-update
  315.8 3.2 convolution_convert_fusion.refs_0_
  319.0 47.8 %shard_map.56 = bf16[8,8,128,128]{3,2,1,0:T(8,128)(2,1)} custom-call(bf16[8,128,128]{2,1,0:T(8,128)(2,1)} %convolution_convert_fusion.refs_0_), custom_call_target="tpu_custom_call" | custom-call | tf_op jit(solution)/shard_map/pallas_call | solution.py:196
  366.8 1.0 iota_compare_fusion
  367.8 2.9 select_reduce_fusion
  370.8 8.2 %fusion = f32[8,768,128]{1,2,0:T(8,128)S(1)} fusion(bf16[8,768,128]{2,1,0:T(8,128)(2,1)} %get-tuple-element.14, pred[768,768]{1,0:T(8,128)(4,1)} %iota_compare_fusion, bf16[8,768,128]{2,1,0:T(8,128)(2,1)} %get-tuple-element.12, bf16[8,768,128]{2,1,0:T(8,128)(2,1)} %get-tuple-element.13), kind=kOutput, calls=%fused_computation.1 | convolution fusion | flops 2425356288 | bytes 8454144 | tf_op jit(solution)/shard_map/hts,hsj->htj/dot_general | solution.py:410
  378.9 0.0 copy-start
  379.0 3.4 multiply_reduce_fusion
  382.4 0.0 copy-done
  382.4 0.4 fusion.6
  382.8 0.8 copy.11.normed_ref
  383.5 15.6 %all-gather.2.cloned.1.call-done.late_ref = bf16[512,4096]{1,0:T(8,128)(2,1)} async-done(((bf16[512,512]{1,0:T(8,128)(2,1)}), bf16[512,4096]{1,0:T(8,128)(2,1)}) %all-gather.2.cloned.1.call-update) | async-done | bytes 4194320 | tf_op jit(solution)/shard_map/all_gather | solution.py:398
  399.2 43.4 %shard_map.57 = bf16[768,1024]{1,0:T(8,128)(2,1)S(1)} custom-call(bf16[768,1024]{1,0:T(8,128)(2,1)S(1)} %copy.11.normed_ref, bf16[512,4096]{1,0:T(8,128)(2,1)} %get-tuple-element.15.w_ref, bf16[512,4096]{1,0:T(8,128)(2,1)} %all-gather.2.cloned.1.call-done.late_ref), custom_call_target="tpu_custom_call" | custom-call | flops 6442450944 | bytes 11534336 | tf_op jit(solution)/shard_map/pallas_call | solution.py:364
  442.5 1.1 copy.13
  (2 shorter events, 0.0 us)
Async XLA Ops:
  6.5 392.6 %all-gather.2.cloned.1.call-start = ((), (), s32[]{:S(2)}) async-start(), calls=%async_computation | async-start | bytes 4718592 | tf_op jit(solution)/shard_map/all_gather | solution.py:398
  378.9 3.4 copy-start
Sparse Core Ops, SparseCore 0:
  315.9 83.1 all-gather.1

commit v5 on v4

--- a/solution.py
+++ b/solution.py
@@ -9,10 +9,6 @@
 
 HEAD_DIM = 128
 MESH = pl.DeviceIdType.MESH
-
-
-def gather_kernel(n, pieces, arrays, *refs):
-    relay(n, pieces, refs[:arrays], refs[arrays : 2 * arrays], *refs[2 * arrays :])
 
 
 def weights_kernel(n, pieces, depth, tokens_ref, w_ref, w_out_ref, query_ref, key_ref, value_ref, w_out_all, w_all, total, *sems):
@@ -188,23 +184,6 @@
     @pl.loop(1, length)
     def _(step):
         along(step, False, lambda c: c.wait_send())
-
-
-def gather(n, identity, pieces, shapes, *blocks):
-    count = len(pieces)
-    anywhere = pl.BlockSpec(memory_space=pl.ANY)
-    return pl.pallas_call(
-        functools.partial(gather_kernel, n, pieces, len(blocks)),
-        out_shape=[jax.ShapeDtypeStruct(s, b.dtype) for s, b in zip(shapes, blocks)],
-        in_specs=[anywhere] * len(blocks),
-        out_specs=[anywhere] * len(blocks),
-        scratch_shapes=[
-            pltpu.SemaphoreType.DMA((3, n, count)),
-            pltpu.SemaphoreType.DMA((n, count)),
-            pltpu.SemaphoreType.DMA((count,)),
-        ],
-        compiler_params=pltpu.CompilerParams(collective_id=identity, has_side_effects=True),
-    )(*blocks)
 
 
 def project_in(tokens, w_qkv, w_out, early):
@@ -260,20 +239,92 @@
     )(tokens, w_qkv, w_out)
 
 
-def gather_states(states):
+def prefix_kernel(n, parts, local_ref, out_ref, mine, paired, came, goes, pair_send, pair_recv, line_send, line_recv):
+    me = lax.axis_index("seq")
+    row, side = me // 2, me % 2
+    pair = row * 2 + 1 - side
+    has_left, has_right = row > 0, row < n // 2 - 1
+    each = local_ref.shape[0] // parts
+
+    barrier = pltpu.get_barrier_semaphore()
+    pl.semaphore_signal(barrier, inc=1, device_id={"seq": pair}, device_id_type=MESH)
+
+    @pl.when(has_left)
+    def _():
+        pl.semaphore_signal(barrier, inc=1, device_id={"seq": me - 2}, device_id_type=MESH)
+
+    @pl.when(has_right)
+    def _():
+        pl.semaphore_signal(barrier, inc=1, device_id={"seq": me + 2}, device_id_type=MESH)
+
+    pl.semaphore_wait(barrier, 1 + has_left.astype(jnp.int32) + has_right.astype(jnp.int32))
+
+    def across(p):
+        span = pl.ds(p * each, each)
+        return pltpu.make_async_remote_copy(
+            src_ref=mine.at[span],
+            dst_ref=paired.at[span],
+            send_sem=pair_send.at[p],
+            recv_sem=pair_recv.at[p],
+            device_id={"seq": pair},
+            device_id_type=MESH,
+        )
+
+    def onward(p):
+        span = pl.ds(p * each, each)
+        return pltpu.make_async_remote_copy(
+            src_ref=goes.at[span],
+            dst_ref=came.at[span],
+            send_sem=line_send.at[p],
+            recv_sem=line_recv.at[p],
+            device_id={"seq": me + 2},
+            device_id_type=MESH,
+        )
+
+    mine[...] = local_ref[...].astype(mine.dtype)
+    for p in range(parts):
+        across(p).start()
+    out_ref[...] = jnp.zeros_like(out_ref)
+    for p in range(parts):
+        span = pl.ds(p * each, each)
+        across(p).wait_recv()
+
+        @pl.when(has_left)
+        def _():
+            onward(p).wait_recv()
+            out_ref[span] = came[span].astype(jnp.float32)
+
+        @pl.when(has_right)
+        def _():
+            total = out_ref[span] + local_ref[span] + paired[span].astype(jnp.float32)
+            goes[span] = total.astype(goes.dtype)
+            onward(p).start()
+
+        @pl.when(side == 1)
+        def _():
+            out_ref[span] = out_ref[span] + paired[span].astype(jnp.float32)
+
+    for p in range(parts):
+        across(p).wait_send()
+
+        @pl.when(has_right)
+        def _():
+            onward(p).wait_send()
+
+
+def sum_earlier(states):
     n = lax.axis_size("seq")
-    heads = states.shape[0]
-    each = heads // 4
-    pieces = [
-        (
-            0,
-            (pl.ds(part * each, each),),
-            lambda owner, part=part: (owner, pl.ds(part * each, each)),
-            part == 0,
-        )
-        for part in range(4)
-    ]
-    return gather(n, 1, pieces, ((n, *states.shape),), states)[0]
+    parts = 4
+    inside = pl.BlockSpec(memory_space=pltpu.VMEM)
+    return pl.pallas_call(
+        functools.partial(prefix_kernel, n, parts),
+        out_shape=jax.ShapeDtypeStruct(states.shape, jnp.float32),
+        in_specs=[inside],
+        out_specs=inside,
+        scratch_shapes=[pltpu.VMEM(states.shape, jnp.bfloat16)] * 4
+        + [pltpu.SemaphoreType.DMA((parts,))] * 4,
+        compiler_params=pltpu.CompilerParams(collective_id=1, has_side_effects=True),
+    )(states)
 
 
 def project_kernel(n, part, normed_ref, w_ref, late_ref, out_ref, core_out, core_in, far_out, far_in, *sems):
@@ -392,16 +443,12 @@
     rows = tokens.shape[0]
     cols = w_qkv.shape[2]
     heads = cols // HEAD_DIM
-    early = w_out.shape[0] // 2
+    early = w_out.shape[0] * 3 // 4
     query, key, value, w_early = project_in(tokens, w_qkv, w_out, early)
     query, w_late = lax.optimization_barrier((query, w_out[early:]))
     w_late = lax.all_gather(w_late, "seq", axis=1, tiled=True)
     local = jnp.einsum("hti,htj->hij", key, value, preferred_element_type=f32)
-    states = gather_states(local.astype(jnp.bfloat16))
-    before = jnp.arange(states.shape[0]) < lax.axis_index("seq")
-    earlier = jnp.sum(
-        jnp.where(before[:, None, None, None], states.astype(f32), 0.0), axis=0
-    )
+    earlier = sum_earlier(local)
     prefix = prior_state + earlier
     scores = jnp.einsum("hti,hsi->hts", query, key, preferred_element_type=f32)
     place = jnp.arange(rows)

time: 451 us -> 443 us (0.982)
  Pallas kernels: 398 us -> 385 us
  waiting for transfers between devices: 15.6 us -> 22.5 us
    pallas_call x1, Pallas kernels: 47.8 us -> 13.9 us  [sum_earlier(): pl.pallas_call(functools.partial(prefix_kernel, n, parts), out_shape=jax....]
    pallas_call x1, Pallas kernels: 307 us -> 328 us  [project_in(): pl.pallas_call(functools.partial(weights_kernel, n, pieces, depth), out_s...]
    all_gather x1, waiting for transfers between devices: 15.6 us -> 22.5 us  [per_device(): w_late = lax.all_gather(w_late, 'seq', axis=1, tiled=True)]
  transfers between devices with their start and end apart: 1 -> 1, of which waited for: 1 -> 1; matrix products, arithmetic and copies ran while one was open for 4% -> 4% of each run, Pallas kernels for 11% -> 3%
where the time goes in v5:
time: 443 us; the launch traced here: 442 us
  Pallas kernels  385 us (87%)
  waiting for transfers between devices  22.5 us (5%)
  matrix products  14.9 us (3%)
  between operations  13.5 us (3%)
  local copies, waits for them, and re-layouts  5.16 us (1%)
    pallas_call x1, Pallas kernels, project_in(): pl.pallas_call(functools.partial(weights_kernel, n, pieces, depth), out_s...  328 us
    pallas_call x1, Pallas kernels, project_and_sum(): pl.pallas_call(functools.partial(project_kernel, n, part), out_shape=jax....  42.7 us
    all_gather x1, waiting for transfers between devices, per_device(): w_late = lax.all_gather(w_late, 'seq', axis=1, tiled=True)  22.5 us
    pallas_call x1, Pallas kernels, sum_earlier(): pl.pallas_call(functools.partial(prefix_kernel, n, parts), out_shape=jax....  13.9 us
  transfers between devices with their start and end apart: 1, of which 1 were waited for; matrix products, arithmetic and copies ran while one was open for 4% of the time, Pallas kernels for 3%

profile of v5, /device:TPU:0, one launch (start us, length us, event | category | flops | bytes accessed | tf_op | source)
XLA Modules:
  0.0 442.3 jit_solution(3162848079656777273)
XLA Ops:
  6.5 0.0 all-gather.2.cloned.1.call-start
  6.5 1.7 slice.3
  8.2 328.3 %shard_map.55 = (bf16[8,768,128]{2,1,0:T(8,128)(2,1)}, bf16[8,768,128]{2,1,0:T(8,128)(2,1)}, bf16[8,768,128]{2,1,0:T(8,128)(2,1)}, bf16[768,4096]{1,0:T(8,128)(2,1)}) custom-call(bf16[768,4096]{1,0:T(8,128)(2,1)} %tokens_ref.1, bf16[3,512,1024]{2,1,0:T(8,128)(2,1)} %w_ref.1, bf16[1024,512]{1,0:T(8,128)(2,1)} %w_out_ref.1), custom_call_target="tpu_custom_call" | custom-call | tf_op jit(solution)/shard_map/pallas_call | solution.py:221
  336.6 0.0 all-gather.2.cloned.1.call-update
  336.6 3.3 fusion.9.local_ref
  339.9 13.9 %shard_map.56 = f32[8,128,128]{2,1,0:T(8,128)} custom-call(f32[8,128,128]{2,1,0:T(8,128)} %fusion.9.local_ref), custom_call_target="tpu_custom_call" | custom-call | tf_op jit(solution)/shard_map/pallas_call | solution.py:319
  353.7 1.0 iota_compare_fusion
  354.7 8.2 %fusion = f32[8,768,128]{1,2,0:T(8,128)S(1)} fusion(bf16[8,768,128]{2,1,0:T(8,128)(2,1)} %get-tuple-element.14, pred[768,768]{1,0:T(8,128)(4,1)} %iota_compare_fusion, bf16[8,768,128]{2,1,0:T(8,128)(2,1)} %get-tuple-element.12, bf16[8,768,128]{2,1,0:T(8,128)(2,1)} %get-tuple-element.13), kind=kOutput, calls=%fused_computation.1 | convolution fusion | flops 2425356288 | bytes 8454144 | tf_op jit(solution)/shard_map/hts,hsj->htj/dot_general | solution.py:457
  362.9 0.0 copy-start.1
  362.9 3.4 multiply_reduce_fusion
  366.4 0.0 copy-done.1
  366.4 0.4 fusion.6
  366.8 0.8 copy.11.normed_ref
  367.5 22.5 %all-gather.2.cloned.1.call-done.late_ref = bf16[256,4096]{1,0:T(8,128)(2,1)} async-done(((bf16[256,512]{1,0:T(8,128)(2,1)}), bf16[256,4096]{1,0:T(8,128)(2,1)}) %all-gather.2.cloned.1.call-update) | async-done | bytes 2097168 | tf_op jit(solution)/shard_map/all_gather | solution.py:449
  390.0 0.0 copy-start
  390.0 1.6 copy-done
  391.6 42.7 %shard_map.57 = bf16[768,1024]{1,0:T(8,128)(2,1)S(1)} custom-call(bf16[768,1024]{1,0:T(8,128)(2,1)S(1)} %copy.11.normed_ref, bf16[768,4096]{1,0:T(8,128)(2,1)} %get-tuple-element.15.w_ref, bf16[256,4096]{1,0:T(8,128)(2,1)S(1)} %copy-done), custom_call_target="tpu_custom_call" | custom-call | flops 6442450944 | bytes 11534336 | tf_op jit(solution)/shard_map/pallas_call | solution.py:415
  434.3 1.1 copy.13
  (1 shorter events, 0.0 us)
Async XLA Ops:
  6.5 383.5 %all-gather.2.cloned.1.call-start = ((), (), s32[]{:S(2)}) async-start(), calls=%async_computation | async-start | bytes 2359296 | tf_op jit(solution)/shard_map/all_gather | solution.py:449
  362.9 3.4 copy-start.1
  390.0 1.6 copy-start
Sparse Core Ops, SparseCore 0:
  336.7 53.3 all-gather.1
